TPU v7x, 32 devices: a whole 2x2x4 slice. The times are simulated.
32 devices in a mesh: section: 4 (over z), dp: 4 (over y, x), head: 2 (over core).
Axes of the slice: x: 2, y: 2, z: 4, core: 2. Of those that a mesh axis runs over, the one named last changes fastest.
Arguments:
- segments: int32 [5, 512], P(None, 'dp'), may hold values from 0 to 15, never falling along the last dimension, each value on 1 to 64 neighbouring positions
- section_input_stream: bfloat16 [4, 512, 2048], P('section', 'dp', 'head'), may hold values from -16 to 16
- entering: bfloat16 [512, 2048], P('dp'), may hold values from -16 to 16
- pending_first_values: bfloat16 [4, 512, 512], P('section', 'dp', 'head'), may hold values from -6 to 6
- norm_gain_vector: float32 [4, 2048], P('section'), may hold values from 0.1 to 1.9
- query_weight: bfloat16 [4, 2048, 2048], P('section', None, 'head'), may hold values from -0.110485435 to 0.110485435
- key_weight: bfloat16 [4, 2048, 512], P('section', None, 'head'), may hold values from -0.110485435 to 0.110485435
- value_weight: bfloat16 [4, 2048, 512], P('section', None, 'head'), may hold values from -0.125 to 0.125
- output_weight: bfloat16 [4, 2048, 2048], P('section', None, 'head'), may hold values from -0.125 to 0.125
- query_key_scale: float32 [4, 16], P('section', 'head'), may hold values from 0.7 to 24
- value_blend_weight: float32 [4, 4], P('section', 'head'), may hold values from 0.3 to 1.5
- value_cotangent_rows: bfloat16 [4, 2, 512, 512], P('section', None, 'dp', 'head'), may hold values from -0.125 to 0.125
Outputs:
- first_round: bfloat16 [4, 512, 2048], P('section', 'dp', 'head')
- second_round: bfloat16 [4, 512, 2048], P('section', 'dp', 'head')
- value_weight_grads: float32 [4, 2048, 512], P('section', 'dp', 'head')
Inputs may be any that keep to these rules, and one draw needn't show every extreme that they name: `segments`: along each row document ids never fall, and a document holds at most half of 128 tokens.
All inputs are finite; a program needn't handle non-finite values.
Results may differ from a plain program's by a relative error of at most 0.018.
Values may be sent and summed in bfloat16 or wider, within the bound.
A program may use at most 64 MiB of HBM per device.

v0:
```python
import math

import jax
import jax.numpy as jnp
from jax import lax
from jax.sharding import PartitionSpec as P

D = 2048
HEAD_WIDTH = 128


epsilon = 1e-06


def passed_along(shard, axis, by):
    peers = lax.axis_size(axis)
    pairs = [(i, i + by) for i in range(peers) if 0 <= i + by < peers]
    return lax.ppermute(shard, axis, pairs)


def rms_rows(values):
    return values * lax.rsqrt(jnp.mean(values * values, axis=-1, keepdims=True) + epsilon)


def attend(
    full_rows,
    segment_row,
    feature_gain,
    query_proj,
    key_proj,
    value_proj,
    scales,
    mixing,
    earlier_values,
    is_first,
):
    tokens = full_rows.shape[0]
    local_heads = query_proj.shape[1] // HEAD_WIDTH
    local_kv = key_proj.shape[1] // HEAD_WIDTH
    group_size = local_heads // local_kv
    normed = (rms_rows(full_rows.astype(jnp.float32)) * feature_gain).astype(jnp.bfloat16)
    queries = jnp.dot(normed, query_proj, preferred_element_type=jnp.float32).reshape(
        tokens, local_kv, group_size, HEAD_WIDTH
    )
    key_rows = jnp.dot(normed, key_proj, preferred_element_type=jnp.float32).reshape(
        tokens, local_kv, HEAD_WIDTH
    )
    values = jnp.dot(normed, value_proj, preferred_element_type=jnp.float32)
    queries = rms_rows(queries)
    key_rows = rms_rows(key_rows)
    own_values = values.astype(jnp.bfloat16)
    blended = (
        values + jnp.repeat(mixing, HEAD_WIDTH)[None, :] * earlier_values.astype(jnp.float32)
    ).astype(jnp.bfloat16)
    mixed_values = jnp.where(is_first, own_values, blended)
    carried = jnp.where(is_first, own_values, earlier_values)
    factor = (scales / math.sqrt(HEAD_WIDTH)).reshape(local_kv, group_size)
    scores = jnp.einsum("qkgd,tkd->kgqt", queries, key_rows) * factor[:, :, None, None]
    positions = jnp.arange(tokens)
    allowed = (positions[:, None] >= positions[None, :]) & (
        segment_row[:, None] == segment_row[None, :]
    )
    scores = jnp.where(allowed, scores, -jnp.inf)
    row_max = jnp.max(scores, axis=-1, keepdims=True)
    exponent = jnp.exp(scores - row_max)
    weights = (exponent / jnp.sum(exponent, axis=-1, keepdims=True)).astype(jnp.bfloat16)
    attended = jnp.einsum(
        "kgqt,tkd->qkgd",
        weights,
        mixed_values.reshape(tokens, local_kv, HEAD_WIDTH),
        preferred_element_type=jnp.float32,
    )
    attended = attended.astype(jnp.bfloat16).reshape(tokens, local_heads * HEAD_WIDTH)
    return (attended, normed, carried)


def collect(piece):
    return lax.all_gather(piece, "head", axis=1, tiled=True)


def grad_term(normed_rows, cotangent):

    def partial_term(first_row, row_count):
        return jnp.einsum("td,tc->dc", normed_rows, cotangent, preferred_element_type=jnp.float32)

    return partial_term


def per_device(
    segments,
    section_input_stream,
    entering,
    pending_first_values,
    norm_gain_vector,
    query_weight,
    key_weight,
    value_weight,
    output_weight,
    query_key_scale,
    value_blend_weight,
    value_cotangent_rows,
):
    section_index = lax.axis_index("section")
    head_index = lax.axis_index("head")
    is_first = section_index == 0
    shard_width = output_weight.shape[2]
    total_batches = segments.shape[0]
    grad_rows = D // lax.axis_size("dp")
    feature_gain = norm_gain_vector[0]
    query_proj = query_weight[0]
    key_proj = key_weight[0]
    value_proj = value_weight[0]
    out_proj = output_weight[0]
    scales = query_key_scale[0]
    mixing = value_blend_weight[0]

    def project(own_rows, attended):
        all_heads = collect(attended)
        return (
            own_rows.astype(jnp.float32)
            + jnp.dot(all_heads, out_proj, preferred_element_type=jnp.float32)
        ).astype(jnp.bfloat16)

    first_segments = lax.dynamic_index_in_dim(segments, section_index, 0, keepdims=False)
    own_first = section_input_stream[0]
    gathered_first = collect(own_first)
    attended_first, normed_first, carried_first = attend(
        gathered_first,
        first_segments,
        feature_gain,
        query_proj,
        key_proj,
        value_proj,
        scales,
        mixing,
        pending_first_values[0],
        is_first,
    )
    output_first = project(own_first, attended_first)
    whole_first = collect(output_first)
    received_whole, received_values = passed_along((whole_first, carried_first), "section", 1)
    gathered_second = jnp.where(is_first, entering, received_whole)
    own_second = lax.dynamic_slice_in_dim(gathered_second, head_index * shard_width, shard_width, 1)
    second_index = (section_index + total_batches - 1) % total_batches
    second_segments = lax.dynamic_index_in_dim(segments, second_index, 0, keepdims=False)
    attended_second, normed_second, carried_second = attend(
        gathered_second,
        second_segments,
        feature_gain,
        query_proj,
        key_proj,
        value_proj,
        scales,
        mixing,
        received_values,
        is_first,
    )
    output_second = project(own_second, attended_second)
    first_term = grad_term(normed_first, value_cotangent_rows[0, 0])
    second_term = grad_term(normed_second, value_cotangent_rows[0, 1])
    first_row = jnp.int32(0)
    gradients = lax.psum_scatter(
        first_term(first_row, grad_rows * lax.axis_size("dp"))
        + second_term(first_row, grad_rows * lax.axis_size("dp")),
        "dp",
        scatter_dimension=0,
        tiled=True,
    )
    return (output_first[None], output_second[None], gradients[None])


def solution(mesh):
    return jax.shard_map(
        per_device,
        mesh=mesh,
        in_specs=(
            P(None, "dp"),
            P("section", "dp", "head"),
            P("dp", None),
            P("section", "dp", "head"),
            P("section", None),
            P("section", None, "head"),
            P("section", None, "head"),
            P("section", None, "head"),
            P("section", None, "head"),
            P("section", "head"),
            P("section", "head"),
            P("section", None, "dp", "head"),
        ),
        out_specs=(
            P("section", "dp", "head"),
            P("section", "dp", "head"),
            P("section", "dp", "head"),
        ),
        check_vma=False,
    )
```

profile of v0, /device:TPU:0, one launch (start us, length us, event | category | flops | bytes accessed | tf_op | source)
XLA Modules:
  0.0 98.1 jit_solution(3976746858789590123)
XLA Ops:
  7.2 0.8 broadcast_bitcast_fusion
  8.0 2.5 %all-gather = bf16[1,128,2048]{2,1,0:T(8,128)(2,1)S(1)} all-gather(bf16[1,128,1024]{2,1,0:T(8,128)(2,1)} %param.13), channel_id=2, replica_groups=mesh['section'=4,'dp'=4,'head'=2] {'head'}, dimensions={2}, use_global_device_ids=true | all-gather | bytes 786432 | tf_op jit(solution)/shard_map/all_gather | solution.py:78
  10.7 1.9 %bitcast_select_fusion = (bf16[128,256]{1,0:T(8,128)(2,1)}, bf16[128,256]{1,0:T(8,128)(2,1)S(1)}) fusion(bf16[1,128,256]{2,1,0:T(8,128)(2,1)} %param.15, pred[]{:T(512)S(6)} %eq.35, f32[256]{0:T(256)S(1)} %broadcast_bitcast_fusion, bf16[1,2048,256]{2,1,0:T(8,128)(2,1)S(1)} %copy-done, bf16[1,128,2048]{2,1,0:T(8,128)(2,1)S(1)} %all-gather, ...), kind=kOutput, calls=%fused_computation.67 | convolution fusion | flops 135495680 | bytes 1779201 | tf_op jit(solution)/shard_map/dot_general | solution.py:48
  12.7 6.5 %copy.44 = bf16[1024,2048]{1,0:T(8,128)(2,1)} copy(bf16[1024,2048]{0,1:T(8,128)(2,1)} %bitcast.142) | data formatting | bytes 8388608 | tf_op jit(solution)/shard_map/dot_general | solution.py:42
  19.2 3.6 %multiply_reduce_fusion.1 = (f32[128,2,4]{0,2,1:T(4,128)S(1)}, f32[128,2,4,128]{0,3,2,1:T(8,128)S(1)}) fusion(bf16[2,4,128,2048]{3,2,1,0:T(8,128)(2,1)} %bitcast.140, f32[2048]{0:T(1024)S(1)} %bitcast.150, f32[128]{0:T(128)S(1)} %add_rsqrt_fusion.5, bf16[1,128,2048]{2,1,0:T(8,128)(2,1)S(1)} %all-gather), kind=kOutput, calls=%fused_computation.49 | convolution fusion | flops 538180608 | bytes 5255680 | tf_op jit(solution)/shard_map/dot_general | solution.py:42
  22.9 0.8 fusion.61
  23.8 1.5 %copy.43 = bf16[256,2048]{1,0:T(8,128)(2,1)} copy(bf16[256,2048]{0,1:T(8,128)(2,1)S(1)} %bitcast.144) | data formatting | bytes 2097152 | tf_op jit(solution)/shard_map/dot_general | solution.py:45
  25.3 1.8 %multiply_reduce_fusion.3 = (f32[128,2]{0,1:T(2,128)S(1)}, f32[128,2,128]{0,2,1:T(8,128)S(1)}) fusion(bf16[2,128,2048]{2,1,0:T(8,128)(2,1)} %bitcast.145, f32[2048]{0:T(1024)S(1)} %bitcast.151, f32[128]{0:T(128)S(1)} %add_rsqrt_fusion.5, bf16[1,128,2048]{2,1,0:T(8,128)(2,1)S(1)} %all-gather), kind=kOutput, calls=%fused_computation.60 | convolution fusion | flops 135331584 | bytes 1713664 | tf_op jit(solution)/shard_map/dot_general | solution.py:45
  27.5 0.3 convolution_convert_fusion.1
  27.8 2.2 %all_gather.13 = bf16[128,2048]{0,1:T(8,128)(2,1)S(1)} all-gather(bf16[128,1024]{0,1:T(8,128)(2,1)S(1)} %bitcast.147), channel_id=1, replica_groups=mesh['section'=4,'dp'=4,'head'=2] {'head'}, dimensions={1}, use_global_device_ids=true | all-gather | bytes 786432 | tf_op jit(solution)/shard_map/all_gather | solution.py:78
  30.0 3.0 %fusion.17 = bf16[128,1024]{1,0:T(8,128)(2,1)S(1)} fusion(bf16[128,2048]{0,1:T(8,128)(2,1)S(1)} %all_gather.13, bf16[1,2048,1024]{2,1,0:T(8,128)(2,1)} %param.20, bf16[1,128,1024]{2,1,0:T(8,128)(2,1)S(1)} %copy-done.1), kind=kOutput, calls=%fused_computation.24 | convolution fusion | flops 537264128 | bytes 5242880 | tf_op jit(solution)/shard_map/dot_general | solution.py:121
  33.0 2.2 %all_gather.14 = bf16[128,2048]{1,0:T(8,128)(2,1)S(1)} all-gather(bf16[128,1024]{1,0:T(8,128)(2,1)S(1)} %fusion.17), channel_id=1, replica_groups=mesh['section'=4,'dp'=4,'head'=2] {'head'}, dimensions={1}, use_global_device_ids=true | all-gather | bytes 786432 | tf_op jit(solution)/shard_map/all_gather | solution.py:78
  35.2 4.9 %collective-permute-start = (bf16[128,2048]{1,0:T(8,128)(2,1)S(1)}, bf16[128,2048]{1,0:T(8,128)(2,1)S(1)}, u32[]{:S(2)}, u32[]{:S(2)}) collective-permute-start(bf16[128,2048]{1,0:T(8,128)(2,1)S(1)} %all_gather.14), channel_id=1, source_target_pairs={{0,8},{8,16},{16,24},{1,9},{9,17},{17,25},{2,10},{10,18},{18,26},{... | collective-permute-start | bytes 1572872 | tf_op jit(solution)/shard_map/ppermute | solution.py:18
  40.1 0.5 fusion.50
  40.6 10.9 %collective-permute-done = bf16[128,2048]{1,0:T(8,128)(2,1)S(1)} collective-permute-done((bf16[128,2048]{1,0:T(8,128)(2,1)S(1)}, bf16[128,2048]{1,0:T(8,128)(2,1)S(1)}, u32[]{:S(2)}, u32[]{:S(2)}) %collective-permute-start) | collective-permute-done | bytes 524320 | tf_op jit(solution)/shard_map/ppermute | solution.py:18
  51.8 1.9 %convolution_add_fusion = f32[2048,256]{1,0:T(8,128)} fusion(f32[2048,256]{1,0:T(8,128)S(1)} %fusion.50, bf16[1,2,128,256]{3,2,1,0:T(8,128)(2,1)S(1)} %copy-done.7, bf16[128,2048]{1,0:T(8,128)(2,1)S(1)} %get-tuple-element.4, f32[128]{0:T(128)S(1)} %add_rsqrt_fusion.4, f32[2048]{0:T(1024)S(1)} %bitcast.153), kind=kOutput, calls=%fused_computation.6 | convolution fusion | flops 135790592 | bytes 4792832 | tf_op jit(solution)/shard_map/td,tc->dc/dot_general | solution.py:84
  53.7 4.4 %collective-permute-start.1 = (bf16[128,256]{1,0:T(8,128)(2,1)S(1)}, bf16[128,256]{1,0:T(8,128)(2,1)S(1)}, u32[]{:S(2)}, u32[]{:S(2)}) collective-permute-start(bf16[128,256]{1,0:T(8,128)(2,1)S(1)} %copy-done.8), channel_id=1, source_target_pairs={{0,8},{8,16},{16,24},{1,9},{9,17},{17,25},{2,10},{10,18},{18,26},{... | collective-permute-start | bytes 196616 | tf_op jit(solution)/shard_map/ppermute | solution.py:18
  58.2 1.8 %collective-permute-done.1 = bf16[128,256]{1,0:T(8,128)(2,1)S(1)} collective-permute-done((bf16[128,256]{1,0:T(8,128)(2,1)S(1)}, bf16[128,256]{1,0:T(8,128)(2,1)S(1)}, u32[]{:S(2)}, u32[]{:S(2)}) %collective-permute-start.1) | collective-permute-done | bytes 65568 | tf_op jit(solution)/shard_map/ppermute | solution.py:18
  60.0 0.4 fusion.48
  60.5 0.5 multiply_reduce_fusion.2
  61.0 3.9 %multiply_reduce_fusion = (f32[128,2,4]{0,2,1:T(4,128)S(1)}, f32[128,2,4,128]{0,3,2,1:T(8,128)S(1)}) fusion(bf16[2,4,128,2048]{3,2,1,0:T(8,128)(2,1)} %bitcast.141, f32[2048]{0:T(1024)S(1)} %bitcast.156, f32[128]{0:T(128)S(1)} %add_rsqrt_fusion.4, bf16[128,2048]{1,0:T(8,128)(2,1)S(1)} %get-tuple-element.4), kind=kOutput, calls=%fused_computation.46 | convolution fusion | flops 538180608 | bytes 5255680 | tf_op jit(solution)/shard_map/dot_general | solution.py:42
  65.7 2.2 %all_gather.15 = bf16[128,2048]{0,1:T(8,128)(2,1)S(1)} all-gather(bf16[128,1024]{0,1:T(8,128)(2,1)S(1)} %bitcast.148), channel_id=1, replica_groups=mesh['section'=4,'dp'=4,'head'=2] {'head'}, dimensions={1}, use_global_device_ids=true | all-gather | bytes 786432 | tf_op jit(solution)/shard_map/all_gather | solution.py:78
  67.8 3.8 %fusion.40 = bf16[1,128,1024]{2,1,0:T(8,128)(2,1)} fusion(bf16[128,2048]{1,0:T(8,128)(2,1)S(1)} %get-tuple-element.4, s32[]{:T(128)S(6)} %select_n.54, bf16[128,2048]{0,1:T(8,128)(2,1)S(1)} %all_gather.15, bf16[1,2048,1024]{2,1,0:T(8,128)(2,1)} %param.20), kind=kOutput, calls=%fused_computation.51 | convolution fusion | flops 537264128 | bytes 5242884 | tf_op jit(solution)/shard_map/dot_general | solution.py:121
  71.6 19.6 %reduce-scatter.2.cloned.1.call-done = f32[512,256]{1,0:T(8,128)} async-done(((f32[2048,256]{1,0:T(8,128)}), f32[512,256]{1,0:T(8,128)}) %reduce-scatter.2.cloned.1.call-update) | async-done | bytes 524304 | tf_op jit(solution)/shard_map/reduce_scatter | solution.py:162
  (41 shorter events, 2.2 us)
Async XLA Ops:
  7.2 3.5 %copy-start = (bf16[1,2048,256]{2,1,0:T(8,128)(2,1)S(1)}, bf16[1,2048,256]{2,1,0:T(8,128)(2,1)}, u32[]{:S(2)}) copy-start(bf16[1,2048,256]{2,1,0:T(8,128)(2,1)} %param.19) | copy-start | bytes 3145732
  7.2 84.0 %reduce-scatter.2.cloned.1.call-start = ((), (), s32[]{:S(2)}) async-start(), calls=%async_computation.1 | async-start | bytes 2621440 | tf_op jit(solution)/shard_map/reduce_scatter | solution.py:162
  12.7 6.5 %copy-start.6 = (f32[1,2048]{1,0:T(1,128)S(1)}, f32[1,2048]{1,0:T(1,128)}, u32[]{:S(2)}) copy-start(f32[1,2048]{1,0:T(1,128)} %param.16) | copy-start | bytes 24580
  19.2 3.6 %copy-start.9 = (f32[1,8]{1,0:T(1,128)S(1)}, f32[1,8]{1,0:T(1,128)}, u32[]{:S(2)}) copy-start(f32[1,8]{1,0:T(1,128)} %param.21) | copy-start | bytes 100
  19.2 4.6 %copy-start.3 = (bf16[1,2048,256]{2,1,0:T(8,128)(2,1)S(1)}, bf16[1,2048,256]{2,1,0:T(8,128)(2,1)}, u32[]{:S(2)}) copy-start(bf16[1,2048,256]{2,1,0:T(8,128)(2,1)} %param.18) | copy-start | bytes 3145732
  23.8 6.2 %copy-start.1 = (bf16[1,128,1024]{2,1,0:T(8,128)(2,1)S(1)}, bf16[1,128,1024]{2,1,0:T(8,128)(2,1)}, u32[]{:S(2)}) copy-start(bf16[1,128,1024]{2,1,0:T(8,128)(2,1)} %param.13) | copy-start | bytes 786436
  27.5 12.6 %copy-start.7 = (bf16[1,2,128,256]{3,2,1,0:T(8,128)(2,1)S(1)}, bf16[1,2,128,256]{3,2,1,0:T(8,128)(2,1)}, u32[]{:S(2)}) copy-start(bf16[1,2,128,256]{3,2,1,0:T(8,128)(2,1)} %param.23) | copy-start | bytes 393220
  30.0 21.5 %copy-start.5 = (bf16[128,2048]{1,0:T(8,128)(2,1)S(1)}, bf16[128,2048]{1,0:T(8,128)(2,1)}, u32[]{:S(2)}) copy-start(bf16[128,2048]{1,0:T(8,128)(2,1)} %param.14) | copy-start | bytes 1572868
  33.0 20.7 %copy-start.2 = (bf16[128,1024]{1,0:T(8,128)(2,1)}, bf16[128,1024]{1,0:T(8,128)(2,1)S(1)}, u32[]{:S(2)}) copy-start(bf16[128,1024]{1,0:T(8,128)(2,1)S(1)} %fusion.17) | copy-start | bytes 786436
  35.2 16.3 %collective-permute-start = (bf16[128,2048]{1,0:T(8,128)(2,1)S(1)}, bf16[128,2048]{1,0:T(8,128)(2,1)S(1)}, u32[]{:S(2)}, u32[]{:S(2)}) collective-permute-start(bf16[128,2048]{1,0:T(8,128)(2,1)S(1)} %all_gather.14), channel_id=1, source_target_pairs={{0,8},{8,16},{16,24},{1,9},{9,17},{17,25},{2,10},{10,18},{18,26},{... | collective-permute-start | bytes 1572872 | tf_op jit(solution)/shard_map/ppermute | solution.py:18
  40.6 13.1 %copy-start.8 = (bf16[128,256]{1,0:T(8,128)(2,1)S(1)}, bf16[128,256]{1,0:T(8,128)(2,1)}, u32[]{:S(2)}) copy-start(bf16[128,256]{1,0:T(8,128)(2,1)} %get-tuple-element.5) | copy-start | bytes 196612
  51.8 8.7 %copy-start.4 = (bf16[256,2048]{1,0:T(8,128)(2,1)S(1)}, bf16[256,2048]{1,0:T(8,128)(2,1)}, u32[]{:S(2)}) copy-start(bf16[256,2048]{1,0:T(8,128)(2,1)} %copy.43) | copy-start | bytes 3145732
  53.7 6.3 %collective-permute-start.1 = (bf16[128,256]{1,0:T(8,128)(2,1)S(1)}, bf16[128,256]{1,0:T(8,128)(2,1)S(1)}, u32[]{:S(2)}, u32[]{:S(2)}) collective-permute-start(bf16[128,256]{1,0:T(8,128)(2,1)S(1)} %copy-done.8), channel_id=1, source_target_pairs={{0,8},{8,16},{16,24},{1,9},{9,17},{17,25},{2,10},{10,18},{18,26},{... | collective-permute-start | bytes 196616 | tf_op jit(solution)/shard_map/ppermute | solution.py:18
Sparse Core Ops, SparseCore 0:
  53.8 37.3 reduce-scatter.1
where the time goes:
time: 98.6 us; the launch traced here: 98.1 us
  waiting for transfers between devices  32.3 us (33%)
  matrix products  22.4 us (23%)
  between operations  14.3 us (15%)
  local copies, waits for them, and re-layouts  9.88 us (10%)
  starting transfers between devices  9.31 us (9%)
  blocking collectives  9.01 us (9%)
    reduce_scatter x1, waiting for transfers between devices, per_device(): lax.psum_scatter(first_term(first_row, grad_rows * lax.axis_size('dp')) +...  19.6 us
    ppermute x2, waiting for transfers between devices, passed_along(): return lax.ppermute(shard, axis, pairs)  12.7 us
    ppermute x2, starting transfers between devices, passed_along(): return lax.ppermute(shard, axis, pairs)  9.28 us
    all_gather x4, blocking collectives, collect(): return lax.all_gather(piece, 'head', axis=1, tiled=True)  9.01 us
    dot_general x2, matrix products, attend(): jnp.dot(normed, query_proj, preferred_element_type=jnp.float32)  7.5 us
    dot_general x2, matrix products, project(): jnp.dot(all_heads, out_proj, preferred_element_type=jnp.float32)  6.79 us
    dot_general x1, local copies, waits for them, and re-layouts, attend(): jnp.dot(normed, query_proj, preferred_element_type=jnp.float32)  6.5 us
    dot_general x2, matrix products, partial_term(): jnp.einsum('td,tc->dc', normed_rows, cotangent, preferred_element_type=jn...  2.41 us
  transfers between devices with their start and end apart: 3, of which 3 were waited for; matrix products, arithmetic and copies ran while one was open for 10% of the time, Pallas kernels for 0%

commit v1 on v0

v1 whole, which is shorter than its diff:
```python
import functools
import math

import jax
import jax.numpy as jnp
from jax import lax
from jax.experimental import pallas as pl
from jax.experimental.pallas import tpu as pltpu
from jax.sharding import PartitionSpec as P

HEAD_WIDTH = 128
CHUNK = 256
EPSILON = 1e-06
F32 = jnp.float32
BF16 = jnp.bfloat16


def rms_rows(values):
    return values * lax.rsqrt(jnp.mean(values * values, axis=-1, keepdims=True) + EPSILON)


def dot(a, b):
    return jnp.dot(a, b, preferred_element_type=F32)


def split_high_low(values):
    high = values.astype(BF16)
    return high, (values - high.astype(F32)).astype(BF16)


def kernel(
    sections,
    replicas,
    heads,
    seg_hbm,
    x_hbm,
    entering_hbm,
    pending_hbm,
    gain_hbm,
    wq_hbm,
    wk_hbm,
    wv_hbm,
    wo_hbm,
    scale_hbm,
    blend_hbm,
    cot_hbm,
    out1_hbm,
    out2_hbm,
    grad_hbm,
    seg,
    gain,
    scale,
    blend,
    wq,
    wk,
    wv,
    wo,
    x1,
    x2,
    f1,
    f2,
    normed1,
    normed2,
    acc,
    att1,
    att2,
    out1,
    out2,
    proj,
    rows_n,
    rows_c,
    grad,
    local_sem,
    weight_sem,
    enter_sem,
    out_sem,
    x_send,
    x_recv,
    c_send,
    c_recv,
    n_send,
    n_recv,
    a_send,
    a_recv,
    z_send,
    z_recv,
    f_send,
    f_recv,
    v_send,
    v_recv,
):
    section = lax.axis_index("section")
    replica = lax.axis_index("dp")
    me = lax.axis_index("head")
    tokens, width = x1.shape[1], x1.shape[2]
    model = width * heads
    q_width, kv_width = wq.shape[1], wk.shape[1]
    kv_heads = kv_width // HEAD_WIDTH
    group = q_width // kv_width
    grad_rows = model // replicas
    chunks = width // CHUNK
    is_first = section == 0
    not_first = section > 0
    not_last = section < sections - 1

    def local(src, dst, sem):
        copy = pltpu.make_async_copy(src, dst, sem)
        copy.start()
        return copy

    def remote(src, dst, send, recv, where):
        return pltpu.make_async_remote_copy(
            src_ref=src,
            dst_ref=dst,
            send_sem=send,
            recv_sem=recv,
            device_id=where,
            device_id_type=pl.DeviceIdType.MESH,
        )

    def head_at(step):
        return lax.rem(me + step, heads)

    def replica_at(step):
        return lax.rem(replica + step, replicas)

    x_load = local(x_hbm.at[0], x1.at[me], local_sem.at[0])
    gain_load = local(gain_hbm, gain, local_sem.at[1])
    wk_load = local(wk_hbm.at[0], wk, weight_sem.at[0])
    wv_load = local(wv_hbm.at[0], wv, weight_sem.at[1])
    quarter = model // 4
    wq_loads = [
        local(
            wq_hbm.at[0, pl.ds(i * quarter, quarter)],
            wq.at[pl.ds(i * quarter, quarter)],
            weight_sem.at[2 + i],
        )
        for i in range(4)
    ]
    seg_load = local(seg_hbm, seg, local_sem.at[2])
    scale_load = local(scale_hbm, scale, local_sem.at[3])
    blend_load = local(blend_hbm, blend, local_sem.at[4])
    cot_load = local(cot_hbm.at[0], rows_c.at[replica], local_sem.at[5])
    f1_load = pltpu.make_async_copy(pending_hbm.at[0], f1, local_sem.at[6])

    @pl.when(not_first)
    def _():
        f1_load.start()

    wo_loads = [
        local(
            wo_hbm.at[0, pl.ds(i * quarter, quarter)],
            wo.at[pl.ds(i * quarter, quarter)],
            weight_sem.at[6 + i],
        )
        for i in range(4)
    ]
    enter_loads = [
        pltpu.make_async_copy(
            entering_hbm.at[:, pl.ds(h * width, width)], x2.at[h], enter_sem.at[h]
        )
        for h in range(heads)
    ]

    @pl.when(is_first)
    def _():
        for load in enter_loads:
            load.start()
        f2[...] = jnp.zeros_like(f2)

    barrier = pltpu.get_barrier_semaphore()

    def greet(where):
        pl.semaphore_signal(barrier, inc=1, device_id=where, device_id_type=pl.DeviceIdType.MESH)

    for step in range(1, heads):
        greet((section, replica, head_at(step)))
    for step in range(1, replicas):
        greet((section, replica_at(step), me))

    @pl.when(not_first)
    def _():
        greet((section - 1, replica, me))

    @pl.when(not_last)
    def _():
        greet((section + 1, replica, me))

    pl.semaphore_wait(
        barrier,
        heads - 1 + replicas - 1 + not_first.astype(jnp.int32) + not_last.astype(jnp.int32),
    )

    x_copies = []
    for step in range(1, heads):
        copy = remote(
            x_hbm.at[0],
            x1.at[me],
            x_send.at[step - 1],
            x_recv.at[step - 1],
            (section, replica, head_at(step)),
        )
        copy.start()
        x_copies.append(copy)
    value_copy = remote(f1, f2, v_send.at[0], v_recv.at[0], (section + 1, replica, me))

    gain_load.wait()
    x_load.wait()
    for copy in x_copies:
        copy.wait_recv()
    squares = jnp.zeros((tokens, 1), F32)
    for h in range(heads):
        part = x1[h].astype(F32)
        squares += jnp.sum(part * part, axis=-1, keepdims=True)
    inverse = lax.rsqrt(squares / model + EPSILON)
    for h in range(heads):
        columns = pl.ds(h * width, width)
        normed1[:, columns] = (x1[h].astype(F32) * inverse * gain[:, columns]).astype(BF16)

    def send_normed(normed, turn):
        copies = []
        for step in range(1, replicas):
            peer = replica_at(step)
            first = pl.multiple_of(peer * grad_rows, 128)
            copy = remote(
                normed.at[:, pl.ds(first, grad_rows)],
                rows_n.at[turn, replica],
                n_send.at[turn, step - 1],
                n_recv.at[turn, step - 1],
                (section, peer, me),
            )
            copy.start()
            copies.append(copy)
        first = pl.multiple_of(replica * grad_rows, 128)
        rows_n[turn, replica] = normed[:, pl.ds(first, grad_rows)]
        return copies

    n1_copies = send_normed(normed1, 0)
    c_copies = []
    for step in range(1, replicas):
        copy = remote(
            cot_hbm.at[0],
            rows_c.at[replica],
            c_send.at[step - 1],
            c_recv.at[step - 1],
            (section, replica_at(step), me),
        )
        copy.start()
        c_copies.append(copy)

    k_at, v_at = q_width, q_width + kv_width
    wk_load.wait()
    acc[:, pl.ds(k_at, kv_width)] = dot(normed1[...], wk[...])
    wv_load.wait()
    acc[:, pl.ds(v_at, kv_width)] = dot(normed1[...], wv[...])
    for load in wq_loads:
        load.wait()

    def query_tile(i, _):
        columns = pl.ds(pl.multiple_of(i * CHUNK, CHUNK), CHUNK)
        acc[:, columns] = dot(normed1[...], wq[:, columns])
        return 0

    lax.fori_loop(0, q_width // CHUNK, query_tile, 0)

    seg_load.wait()
    scale_load.wait()
    blend_load.wait()

    @pl.when(not_first)
    def _():
        f1_load.wait()

    @pl.when(is_first)
    def _():
        f1[...] = acc[:, pl.ds(v_at, kv_width)].astype(BF16)

    @pl.when(not_last)
    def _():
        value_copy.start()

    causal = lax.broadcasted_iota(jnp.int32, (tokens, tokens), 0) >= lax.broadcasted_iota(
        jnp.int32, (tokens, tokens), 1
    )

    def attend(segment_index, earlier, att, turn):
        row = seg[pl.ds(segment_index, 1), :].astype(F32)
        across = jnp.broadcast_to(row, (tokens, tokens))
        allowed = causal & (across == across.T)
        for g in range(kv_heads):
            kv_columns = pl.ds(g * HEAD_WIDTH, HEAD_WIDTH)
            values = acc[:, pl.ds(v_at + g * HEAD_WIDTH, HEAD_WIDTH)]
            blended = values + blend[:, g : g + 1] * earlier[:, kv_columns].astype(F32)
            mixed_values = jnp.where(is_first, values, blended).astype(BF16)
            key_high, key_low = split_high_low(
                rms_rows(acc[:, pl.ds(k_at + g * HEAD_WIDTH, HEAD_WIDTH)])
            )
            keys = jnp.concatenate([key_high, key_high, key_low], axis=1)
            queries = []
            for j in range(group):
                h = g * group + j
                query_high, query_low = split_high_low(
                    rms_rows(acc[:, pl.ds(h * HEAD_WIDTH, HEAD_WIDTH)])
                    * (scale[:, h : h + 1] / math.sqrt(HEAD_WIDTH))
                )
                queries.append(jnp.concatenate([query_high, query_low, query_high], axis=1))
            scores = lax.dot_general(
                jnp.concatenate(queries, axis=0),
                keys,
                (((1,), (1,)), ((), ())),
                preferred_element_type=F32,
            ).reshape(group, tokens, tokens)
            scores = jnp.where(allowed[None], scores, -1e30)
            exponent = jnp.exp(scores - jnp.max(scores, axis=-1, keepdims=True))
            weights = (exponent / jnp.sum(exponent, axis=-1, keepdims=True)).astype(BF16)
            result = dot(weights.reshape(group * tokens, tokens), mixed_values).astype(BF16)
            for j in range(group):
                att[me, :, pl.ds((g * group + j) * HEAD_WIDTH, HEAD_WIDTH)] = result[
                    j * tokens : (j + 1) * tokens
                ]
            columns = pl.ds(g * group * HEAD_WIDTH, group * HEAD_WIDTH)
            for step in range(1, heads):
                copy = remote(
                    att.at[me, :, columns],
                    att.at[me, :, columns],
                    a_send.at[turn, step - 1, g],
                    a_recv.at[turn, step - 1, g],
                    (section, replica, head_at(step)),
                )
                copy.start()
                a_copies.append((turn, copy))

    a_copies = []
    attend(section, f1, att1, 0)

    def own_part(att):
        rows = pl.ds(pl.multiple_of(me * q_width, q_width), q_width)

        def tile(i, _):
            columns = pl.ds(pl.multiple_of(i * CHUNK, CHUNK), CHUNK)
            proj[:, columns] = dot(att[me], wo[rows, columns])
            return 0

        lax.fori_loop(0, chunks, tile, 0)

    def whole_tile(att, stream, columns):
        total = proj[:, columns] + stream[me, :, columns].astype(F32)
        for step in range(1, heads):
            peer = lax.rem(me + heads - step, heads)
            rows = pl.ds(pl.multiple_of(peer * q_width, q_width), q_width)
            total += dot(att[peer], wo[rows, columns])
        return total.astype(BF16)

    def z_copy(c):
        columns = pl.ds(c * CHUNK, CHUNK)
        return remote(
            out1.at[:, columns],
            x2.at[me, :, columns],
            z_send.at[c],
            z_recv.at[c],
            (section + 1, replica, me),
        )

    for load in wo_loads:
        load.wait()
    own_part(att1)
    for turn, copy in a_copies:
        if turn == 0:
            copy.wait_recv()
    for c in range(chunks):
        columns = pl.ds(c * CHUNK, CHUNK)
        out1[:, columns] = whole_tile(att1, x1, columns)

        @pl.when(not_last)
        def _(c=c):
            z_copy(c).start()

    out1_store = local(out1, out1_hbm.at[0], out_sem.at[0])

    cot_load.wait()
    for copy in c_copies + n1_copies:
        copy.wait_recv()

    def grad_part(turn):
        total = jnp.zeros(grad.shape, F32)
        for p in range(replicas):
            total += lax.dot_general(
                rows_n[turn, p],
                rows_c[p, turn],
                (((0,), (0,)), ((), ())),
                preferred_element_type=F32,
            )
        return total

    grad[...] = grad_part(0)

    def forward(step, c):
        columns = pl.ds(c * CHUNK, CHUNK)
        return remote(
            x2.at[me, :, columns],
            x2.at[me, :, columns],
            f_send.at[step - 1, c],
            f_recv.at[step - 1, c],
            (section, replica, head_at(step)),
        )

    @pl.when(is_first)
    def _():
        for load in enter_loads:
            load.wait()

    squares = jnp.zeros((tokens, 1), F32)
    for c in range(chunks):
        columns = pl.ds(c * CHUNK, CHUNK)

        @pl.when(not_first)
        def _(c=c):
            z_copy(c).wait_recv()
            for step in range(1, heads):
                forward(step, c).start()

        for step in range(heads):
            owner = lax.rem(me + heads - step, heads)
            if step > 0:

                @pl.when(not_first)
                def _(step=step, c=c):
                    forward(step, c).wait_recv()

            rows = pl.ds(pl.multiple_of(owner * width + c * CHUNK, CHUNK), CHUNK)
            part = x2[owner, :, columns].astype(F32)
            squares += jnp.sum(part * part, axis=-1, keepdims=True)
            scaled = (part * gain[:, rows]).astype(BF16)
            for weight, at, size in (
                (wk, k_at, kv_width),
                (wv, v_at, kv_width),
                (wq, 0, q_width),
            ):
                product = dot(scaled, weight[rows, :])
                if c == 0 and step == 0:
                    acc[:, pl.ds(at, size)] = product
                else:
                    acc[:, pl.ds(at, size)] += product
    inverse = lax.rsqrt(squares / model + EPSILON)
    for h in range(heads):
        columns = pl.ds(h * width, width)
        normed2[:, columns] = (x2[h].astype(F32) * inverse * gain[:, columns]).astype(BF16)
    n2_copies = send_normed(normed2, 1)
    acc[...] = acc[...] * inverse

    @pl.when(not_first)
    def _():
        value_copy.wait_recv()

    attend(lax.rem(section + sections, sections + 1), f2, att2, 1)
    own_part(att2)
    for turn, copy in a_copies:
        if turn == 1:
            copy.wait_recv()
    for c in range(chunks):
        columns = pl.ds(c * CHUNK, CHUNK)
        out2[:, columns] = whole_tile(att2, x2, columns)
    out2_store = local(out2, out2_hbm.at[0], out_sem.at[1])

    for copy in n2_copies:
        copy.wait_recv()
    grad[...] += grad_part(1)
    grad_store = local(grad, grad_hbm.at[0], out_sem.at[2])

    for copy in x_copies + c_copies + n1_copies + n2_copies:
        copy.wait_send()
    for _, copy in a_copies:
        copy.wait_send()

    @pl.when(not_last)
    def _():
        value_copy.wait_send()
        for c in range(chunks):
            z_copy(c).wait_send()

    @pl.when(not_first)
    def _():
        for c in range(chunks):
            for step in range(1, heads):
                forward(step, c).wait_send()

    out1_store.wait()
    out2_store.wait()
    grad_store.wait()


def solution(mesh):
    sections, replicas, heads = (mesh.shape[a] for a in ("section", "dp", "head"))

    def per_device(
        segments,
        stream,
        entering,
        pending,
        gain,
        wq,
        wk,
        wv,
        wo,
        scale,
        blend,
        cotangent,
    ):
        _, tokens, width = stream.shape
        model = width * heads
        q_width, kv_width = wq.shape[2], wk.shape[2]
        grad_rows = model // replicas
        chunks = width // CHUNK
        kv_heads = kv_width // HEAD_WIDTH
        others = heads - 1
        peers = replicas - 1
        dma = pltpu.SemaphoreType.DMA
        scratch = [
            pltpu.VMEM(segments.shape, jnp.int32),
            pltpu.VMEM(gain.shape, F32),
            pltpu.VMEM(scale.shape, F32),
            pltpu.VMEM(blend.shape, F32),
            pltpu.VMEM((model, q_width), BF16),
            pltpu.VMEM((model, kv_width), BF16),
            pltpu.VMEM((model, kv_width), BF16),
            pltpu.VMEM((model, width), BF16),
            pltpu.VMEM((heads, tokens, width), BF16),
            pltpu.VMEM((heads, tokens, width), BF16),
            pltpu.VMEM((tokens, kv_width), BF16),
            pltpu.VMEM((tokens, kv_width), BF16),
            pltpu.VMEM((tokens, model), BF16),
            pltpu.VMEM((tokens, model), BF16),
            pltpu.VMEM((tokens, q_width + 2 * kv_width), F32),
            pltpu.VMEM((heads, tokens, q_width), BF16),
            pltpu.VMEM((heads, tokens, q_width), BF16),
            pltpu.VMEM((tokens, width), BF16),
            pltpu.VMEM((tokens, width), BF16),
            pltpu.VMEM((tokens, width), F32),
            pltpu.VMEM((2, replicas, tokens, grad_rows), BF16),
            pltpu.VMEM((replicas, 2, tokens, kv_width), BF16),
            pltpu.VMEM((grad_rows, kv_width), F32),
            dma((7,)),
            dma((10,)),
            dma((heads,)),
            dma((3,)),
            dma((others,)),
            dma((others,)),
            dma((peers,)),
            dma((peers,)),
            dma((2, peers)),
            dma((2, peers)),
            dma((2, others, kv_heads)),
            dma((2, others, kv_heads)),
            dma((chunks,)),
            dma((chunks,)),
            dma((others, chunks)),
            dma((others, chunks)),
            dma((1,)),
            dma((1,)),
        ]
        return pl.pallas_call(
            functools.partial(kernel, sections, replicas, heads),
            out_shape=(
                jax.ShapeDtypeStruct(stream.shape, BF16),
                jax.ShapeDtypeStruct(stream.shape, BF16),
                jax.ShapeDtypeStruct((1, grad_rows, kv_width), F32),
            ),
            in_specs=[pl.BlockSpec(memory_space=pl.ANY)] * 12,
            out_specs=(pl.BlockSpec(memory_space=pl.ANY),) * 3,
            scratch_shapes=scratch,
            compiler_params=pltpu.CompilerParams(
                collective_id=0, has_side_effects=True, vmem_limit_bytes=56 * 1024 * 1024
            ),
        )(
            segments,
            stream,
            entering,
            pending,
            gain,
            wq,
            wk,
            wv,
            wo,
            scale,
            blend,
            cotangent,
        )

    return jax.shard_map(
        per_device,
        mesh=mesh,
        in_specs=(
            P(None, "dp"),
            P("section", "dp", "head"),
            P("dp", None),
            P("section", "dp", "head"),
            P("section", None),
            P("section", None, "head"),
            P("section", None, "head"),
            P("section", None, "head"),
            P("section", None, "head"),
            P("section", "head"),
            P("section", "head"),
            P("section", None, "dp", "head"),
        ),
        out_specs=(
            P("section", "dp", "head"),
            P("section", "dp", "head"),
            P("section", "dp", "head"),
        ),
        check_vma=False,
    )
```

time: 98.6 us -> 38.6 us (0.39)
  the two profiles are of different devices: /device:TPU:0 before, /device:TPU:17 now
where the time goes in v1:
time: 38.6 us; the launch traced here: 38.2 us
  Pallas kernels  32.3 us (84%)
  local copies, waits for them, and re-layouts  5.21 us (13%)
  between operations  0.64 us (2%)
    pallas_call x1, Pallas kernels, per_device(): pl.pallas_call(functools.partial(kernel, sections, replicas, heads), out_...  32.3 us
    unnamed x3, local copies, waits for them, and re-layouts  5.21 us

profile of v1, /device:TPU:17, one launch (start us, length us, event | category | flops | bytes accessed | tf_op | source)
XLA Modules:
  0.0 38.2 jit_solution(15291564561875872063)
XLA Ops:
  0.6 32.3 %shard_map.139 = (bf16[1,128,1024]{2,1,0:T(8,128)(2,1)}, bf16[1,128,1024]{2,1,0:T(8,128)(2,1)}, f32[1,512,256]{2,1,0:T(8,128)}) custom-call(s32[5,128]{1,0:T(8,128)} %seg_hbm.1, bf16[1,128,1024]{2,1,0:T(8,128)(2,1)} %x_hbm.1, bf16[128,2048]{1,0:T(8,128)(2,1)} %entering_hbm.1, bf16[1,128,256]{2,1,0:T(8,128)(2,1)} %pending_hbm.1, f32[1,2048]{1,0:T(1,128)} %gain_hbm.1, ...), custom_call_target="tpu_custom_call" | custom-call | tf_op jit(solution)/shard_map/pallas_call | solution.py:561
  32.9 1.7 %copy.18 = bf16[1,128,1024]{2,1,0:T(8,128)(2,1)} copy(bf16[1,128,1024]{2,1,0:T(8,128)(2,1)} %get-tuple-element.6) | data formatting | bytes 524288
  34.6 1.7 %copy.19 = bf16[1,128,1024]{2,1,0:T(8,128)(2,1)} copy(bf16[1,128,1024]{2,1,0:T(8,128)(2,1)} %get-tuple-element.7) | data formatting | bytes 524288
  36.3 1.9 %copy.20 = f32[1,512,256]{2,1,0:T(8,128)} copy(f32[1,512,256]{2,1,0:T(8,128)} %get-tuple-element.8) | data formatting | bytes 1048576

commit v2 on v1

--- a/solution.py
+++ b/solution.py
@@ -13,10 +13,6 @@
 EPSILON = 1e-06
 F32 = jnp.float32
 BF16 = jnp.bfloat16
-
-
-def rms_rows(values):
-    return values * lax.rsqrt(jnp.mean(values * values, axis=-1, keepdims=True) + EPSILON)
 
 
 def dot(a, b):
@@ -204,18 +200,37 @@
         x_copies.append(copy)
     value_copy = remote(f1, f2, v_send.at[0], v_recv.at[0], (section + 1, replica, me))
 
-    gain_load.wait()
-    x_load.wait()
-    for copy in x_copies:
-        copy.wait_recv()
-    squares = jnp.zeros((tokens, 1), F32)
-    for h in range(heads):
-        part = x1[h].astype(F32)
-        squares += jnp.sum(part * part, axis=-1, keepdims=True)
-    inverse = lax.rsqrt(squares / model + EPSILON)
-    for h in range(heads):
-        columns = pl.ds(h * width, width)
-        normed1[:, columns] = (x1[h].astype(F32) * inverse * gain[:, columns]).astype(BF16)
+    c_copies = []
+    for step in range(1, replicas):
+        copy = remote(
+            cot_hbm.at[0],
+            rows_c.at[replica],
+            c_send.at[step - 1],
+            c_recv.at[step - 1],
+            (section, replica_at(step), me),
+        )
+        copy.start()
+        c_copies.append(copy)
+
+    k_at, v_at = q_width, q_width + kv_width
+    weights_at = ((wk, k_at, kv_width), (wv, v_at, kv_width), (wq, 0, q_width))
+
+    def project(part, first_row, size, is_start):
+        rows = pl.ds(pl.multiple_of(first_row, CHUNK), size)
+        scaled = (part * gain[:, rows]).astype(BF16)
+        for weight, at, columns in weights_at:
+            product = dot(scaled, weight[rows, :])
+            if is_start:
+                acc[:, pl.ds(at, columns)] = product
+            else:
+                acc[:, pl.ds(at, columns)] += product
+
+    def normalize(stream, squares, normed):
+        inverse = lax.rsqrt(squares / model + EPSILON)
+        for h in range(heads):
+            columns = pl.ds(h * width, width)
+            normed[:, columns] = (stream[h].astype(F32) * inverse * gain[:, columns]).astype(BF16)
+        return inverse
 
     def send_normed(normed, turn):
         copies = []
@@ -235,33 +250,25 @@
         rows_n[turn, replica] = normed[:, pl.ds(first, grad_rows)]
         return copies
 
-    n1_copies = send_normed(normed1, 0)
-    c_copies = []
-    for step in range(1, replicas):
-        copy = remote(
-            cot_hbm.at[0],
-            rows_c.at[replica],
-            c_send.at[step - 1],
-            c_recv.at[step - 1],
-            (section, replica_at(step), me),
-        )
-        copy.start()
-        c_copies.append(copy)
-
-    k_at, v_at = q_width, q_width + kv_width
+    gain_load.wait()
+    x_load.wait()
     wk_load.wait()
-    acc[:, pl.ds(k_at, kv_width)] = dot(normed1[...], wk[...])
     wv_load.wait()
-    acc[:, pl.ds(v_at, kv_width)] = dot(normed1[...], wv[...])
     for load in wq_loads:
         load.wait()
-
-    def query_tile(i, _):
-        columns = pl.ds(pl.multiple_of(i * CHUNK, CHUNK), CHUNK)
-        acc[:, columns] = dot(normed1[...], wq[:, columns])
-        return 0
-
-    lax.fori_loop(0, q_width // CHUNK, query_tile, 0)
+    part = x1[me].astype(F32)
+    squares = jnp.sum(part * part, axis=-1, keepdims=True)
+    project(part, me * width, width, True)
+    for copy in x_copies:
+        copy.wait_recv()
+    for step in range(1, heads):
+        part = x1[lax.rem(me + heads - step, heads)].astype(F32)
+        squares += jnp.sum(part * part, axis=-1, keepdims=True)
+    inverse1 = normalize(x1, squares, normed1)
+    n1_copies = send_normed(normed1, 0)
+    for step in range(1, heads):
+        owner = lax.rem(me + heads - step, heads)
+        project(x1[owner].astype(F32), owner * width, width, False)
 
     seg_load.wait()
     scale_load.wait()
@@ -273,7 +280,7 @@
 
     @pl.when(is_first)
     def _():
-        f1[...] = acc[:, pl.ds(v_at, kv_width)].astype(BF16)
+        f1[...] = (acc[:, pl.ds(v_at, kv_width)] * inverse1).astype(BF16)
 
     @pl.when(not_last)
     def _():
@@ -283,24 +290,31 @@
         jnp.int32, (tokens, tokens), 1
     )
 
-    def attend(segment_index, earlier, att, turn):
+    ones = jnp.ones((2 * HEAD_WIDTH, HEAD_WIDTH), BF16)
+    mixed_ones = jnp.ones((tokens, HEAD_WIDTH), BF16)
+
+    def unit_rows(values):
+        total = dot(jnp.concatenate(split_high_low(values * values), axis=1), ones)
+        return values * lax.rsqrt(total / HEAD_WIDTH + EPSILON)
+
+    def attend(segment_index, earlier, att, turn, inverse):
         row = seg[pl.ds(segment_index, 1), :].astype(F32)
         across = jnp.broadcast_to(row, (tokens, tokens))
         allowed = causal & (across == across.T)
         for g in range(kv_heads):
             kv_columns = pl.ds(g * HEAD_WIDTH, HEAD_WIDTH)
-            values = acc[:, pl.ds(v_at + g * HEAD_WIDTH, HEAD_WIDTH)]
+            values = acc[:, pl.ds(v_at + g * HEAD_WIDTH, HEAD_WIDTH)] * inverse
             blended = values + blend[:, g : g + 1] * earlier[:, kv_columns].astype(F32)
             mixed_values = jnp.where(is_first, values, blended).astype(BF16)
             key_high, key_low = split_high_low(
-                rms_rows(acc[:, pl.ds(k_at + g * HEAD_WIDTH, HEAD_WIDTH)])
+                unit_rows(acc[:, pl.ds(k_at + g * HEAD_WIDTH, HEAD_WIDTH)] * inverse)
             )
             keys = jnp.concatenate([key_high, key_high, key_low], axis=1)
             queries = []
             for j in range(group):
                 h = g * group + j
                 query_high, query_low = split_high_low(
-                    rms_rows(acc[:, pl.ds(h * HEAD_WIDTH, HEAD_WIDTH)])
+                    unit_rows(acc[:, pl.ds(h * HEAD_WIDTH, HEAD_WIDTH)] * inverse)
                     * (scale[:, h : h + 1] / math.sqrt(HEAD_WIDTH))
                 )
                 queries.append(jnp.concatenate([query_high, query_low, query_high], axis=1))
@@ -311,9 +325,12 @@
                 preferred_element_type=F32,
             ).reshape(group, tokens, tokens)
             scores = jnp.where(allowed[None], scores, -1e30)
-            exponent = jnp.exp(scores - jnp.max(scores, axis=-1, keepdims=True))
-            weights = (exponent / jnp.sum(exponent, axis=-1, keepdims=True)).astype(BF16)
-            result = dot(weights.reshape(group * tokens, tokens), mixed_values).astype(BF16)
+            exponent = jnp.exp(scores - jnp.max(scores, axis=-1, keepdims=True)).astype(BF16)
+            result = dot(
+                exponent.reshape(group * tokens, tokens),
+                jnp.concatenate([mixed_values, mixed_ones], axis=1),
+            )
+            result = (result[:, :HEAD_WIDTH] / result[:, HEAD_WIDTH:]).astype(BF16)
             for j in range(group):
                 att[me, :, pl.ds((g * group + j) * HEAD_WIDTH, HEAD_WIDTH)] = result[
                     j * tokens : (j + 1) * tokens
@@ -331,19 +348,15 @@
                 a_copies.append((turn, copy))
 
     a_copies = []
-    attend(section, f1, att1, 0)
-
-    def own_part(att):
+    attend(section, f1, att1, 0, inverse1)
+
+    def own_tile(att, c):
         rows = pl.ds(pl.multiple_of(me * q_width, q_width), q_width)
-
-        def tile(i, _):
-            columns = pl.ds(pl.multiple_of(i * CHUNK, CHUNK), CHUNK)
-            proj[:, columns] = dot(att[me], wo[rows, columns])
-            return 0
-
-        lax.fori_loop(0, chunks, tile, 0)
-
-    def whole_tile(att, stream, columns):
+        columns = pl.ds(c * CHUNK, CHUNK)
+        proj[:, columns] = dot(att[me], wo[rows, columns])
+
+    def whole_tile(att, stream, c):
+        columns = pl.ds(c * CHUNK, CHUNK)
         total = proj[:, columns] + stream[me, :, columns].astype(F32)
         for step in range(1, heads):
             peer = lax.rem(me + heads - step, heads)
@@ -363,13 +376,16 @@
 
     for load in wo_loads:
         load.wait()
-    own_part(att1)
+    ahead = chunks // 2
+    for c in range(ahead):
+        own_tile(att1, c)
     for turn, copy in a_copies:
         if turn == 0:
             copy.wait_recv()
     for c in range(chunks):
-        columns = pl.ds(c * CHUNK, CHUNK)
-        out1[:, columns] = whole_tile(att1, x1, columns)
+        if c >= ahead:
+            own_tile(att1, c)
+        out1[:, pl.ds(c * CHUNK, CHUNK)] = whole_tile(att1, x1, c)
 
         @pl.when(not_last)
         def _(c=c):
@@ -377,22 +393,17 @@
 
     out1_store = local(out1, out1_hbm.at[0], out_sem.at[0])
 
+    def grad_part(turn, step):
+        p = lax.rem(replica + replicas - step, replicas)
+        return lax.dot_general(
+            rows_n[turn, p],
+            rows_c[p, turn],
+            (((0,), (0,)), ((), ())),
+            preferred_element_type=F32,
+        )
+
     cot_load.wait()
-    for copy in c_copies + n1_copies:
-        copy.wait_recv()
-
-    def grad_part(turn):
-        total = jnp.zeros(grad.shape, F32)
-        for p in range(replicas):
-            total += lax.dot_general(
-                rows_n[turn, p],
-                rows_c[p, turn],
-                (((0,), (0,)), ((), ())),
-                preferred_element_type=F32,
-            )
-        return total
-
-    grad[...] = grad_part(0)
+    grad[...] = grad_part(0, 0)
 
     def forward(step, c):
         columns = pl.ds(c * CHUNK, CHUNK)
@@ -419,52 +430,49 @@
             for step in range(1, heads):
                 forward(step, c).start()
 
-        for step in range(heads):
+        part = x2[me, :, columns].astype(F32)
+        squares += jnp.sum(part * part, axis=-1, keepdims=True)
+        project(part, me * width + c * CHUNK, CHUNK, c == 0)
+        if c < chunks - 1:
+            for step in range(1 + c * (replicas - 1) // (chunks - 1), 1 + (c + 1) * (replicas - 1) // (chunks - 1)):
+                c_copies[step - 1].wait_recv()
+                n1_copies[step - 1].wait_recv()
+                grad[...] += grad_part(0, step)
+
+        @pl.when(not_first)
+        def _(c=c):
+            for step in range(1, heads):
+                forward(step, c).wait_recv()
+
+        parts = [x2[lax.rem(me + heads - step, heads), :, columns].astype(F32) for step in range(1, heads)]
+        for part in parts:
+            squares += jnp.sum(part * part, axis=-1, keepdims=True)
+        if c == chunks - 1:
+            inverse2 = normalize(x2, squares, normed2)
+            n2_copies = send_normed(normed2, 1)
+        for step in range(1, heads):
             owner = lax.rem(me + heads - step, heads)
-            if step > 0:
-
-                @pl.when(not_first)
-                def _(step=step, c=c):
-                    forward(step, c).wait_recv()
-
-            rows = pl.ds(pl.multiple_of(owner * width + c * CHUNK, CHUNK), CHUNK)
-            part = x2[owner, :, columns].astype(F32)
-            squares += jnp.sum(part * part, axis=-1, keepdims=True)
-            scaled = (part * gain[:, rows]).astype(BF16)
-            for weight, at, size in (
-                (wk, k_at, kv_width),
-                (wv, v_at, kv_width),
-                (wq, 0, q_width),
-            ):
-                product = dot(scaled, weight[rows, :])
-                if c == 0 and step == 0:
-                    acc[:, pl.ds(at, size)] = product
-                else:
-                    acc[:, pl.ds(at, size)] += product
-    inverse = lax.rsqrt(squares / model + EPSILON)
-    for h in range(heads):
-        columns = pl.ds(h * width, width)
-        normed2[:, columns] = (x2[h].astype(F32) * inverse * gain[:, columns]).astype(BF16)
-    n2_copies = send_normed(normed2, 1)
-    acc[...] = acc[...] * inverse
+            project(parts[step - 1], owner * width + c * CHUNK, CHUNK, False)
 
     @pl.when(not_first)
     def _():
         value_copy.wait_recv()
 
-    attend(lax.rem(section + sections, sections + 1), f2, att2, 1)
-    own_part(att2)
+    attend(lax.rem(section + sections, sections + 1), f2, att2, 1, inverse2)
+    for c in range(chunks):
+        own_tile(att2, c)
     for turn, copy in a_copies:
         if turn == 1:
             copy.wait_recv()
     for c in range(chunks):
-        columns = pl.ds(c * CHUNK, CHUNK)
-        out2[:, columns] = whole_tile(att2, x2, columns)
+        out2[:, pl.ds(c * CHUNK, CHUNK)] = whole_tile(att2, x2, c)
     out2_store = local(out2, out2_hbm.at[0], out_sem.at[1])
 
-    for copy in n2_copies:
-        copy.wait_recv()
-    grad[...] += grad_part(1)
+    total = grad[...] + grad_part(1, 0)
+    for step in range(1, replicas):
+        n2_copies[step - 1].wait_recv()
+        total += grad_part(1, step)
+    grad[...] = total
     grad_store = local(grad, grad_hbm.at[0], out_sem.at[2])
 
     for copy in x_copies + c_copies + n1_copies + n2_copies:
@@ -487,6 +495,22 @@
     out1_store.wait()
     out2_store.wait()
     grad_store.wait()
+
+
+def store_kernel(*refs):
+    sources, targets, sems = refs[:3], refs[3:6], refs[6]
+    copies = []
+    for source, target in zip(sources, targets):
+        rows = source.shape[1] // 2
+        for i in range(2):
+            block = pl.ds(i * rows, rows)
+            copy = pltpu.make_async_copy(
+                source.at[0, block], target.at[0, block], sems.at[len(copies)]
+            )
+            copy.start()
+            copies.append(copy)
+    for copy in copies:
+        copy.wait()
 
 
 def solution(mesh):
@@ -558,7 +582,7 @@
             dma((1,)),
             dma((1,)),
         ]
-        return pl.pallas_call(
+        results = pl.pallas_call(
             functools.partial(kernel, sections, replicas, heads),
             out_shape=(
                 jax.ShapeDtypeStruct(stream.shape, BF16),
@@ -585,6 +609,14 @@
             blend,
             cotangent,
         )
+        return pl.pallas_call(
+            store_kernel,
+            out_shape=tuple(jax.ShapeDtypeStruct(r.shape, r.dtype) for r in results),
+            in_specs=[pl.BlockSpec(memory_space=pl.ANY)] * 3,
+            out_specs=(pl.BlockSpec(memory_space=pl.ANY),) * 3,
+            scratch_shapes=[dma((6,))],
+            compiler_params=pltpu.CompilerParams(vmem_limit_bytes=56 * 1024 * 1024),
+        )(*results)
 
     return jax.shard_map(
         per_device,

time: 38.6 us -> 61.1 us (1.58)
  Pallas kernels: 32.3 us -> 60.3 us
  local copies, waits for them, and re-layouts: 5.21 us -> 0 us
    pallas_call x0 -> x1, Pallas kernels: none -> 32.9 us  [per_device(): pl.pallas_call(store_kernel, out_shape=tuple((jax.ShapeDtypeStruct(r.shap...]
    unnamed x3 -> x0, local copies, waits for them, and re-layouts: 5.21 us -> none
    pallas_call x1, Pallas kernels: 32.3 us -> 27.4 us  [per_device(): pl.pallas_call(functools.partial(kernel, sections, replicas, heads), out_...]
where the time goes in v2:
time: 61.1 us; the launch traced here: 61 us
  Pallas kernels  60.3 us (99%)
  between operations  0.64 us (1%)
    pallas_call x1, Pallas kernels, per_device(): pl.pallas_call(store_kernel, out_shape=tuple((jax.ShapeDtypeStruct(r.shap...  32.9 us
    pallas_call x1, Pallas kernels, per_device(): pl.pallas_call(functools.partial(kernel, sections, replicas, heads), out_...  27.4 us

profile of v2, /device:TPU:17, one launch (start us, length us, event | category | flops | bytes accessed | tf_op | source)
XLA Modules:
  0.0 61.0 jit_solution(16919943735915473217)
XLA Ops:
  0.6 27.4 %shard_map.139 = (bf16[1,128,1024]{2,1,0:T(8,128)(2,1)}, bf16[1,128,1024]{2,1,0:T(8,128)(2,1)}, f32[1,512,256]{2,1,0:T(8,128)}) custom-call(s32[5,128]{1,0:T(8,128)} %seg_hbm.1, bf16[1,128,1024]{2,1,0:T(8,128)(2,1)} %x_hbm.1, bf16[128,2048]{1,0:T(8,128)(2,1)} %entering_hbm.1, bf16[1,128,256]{2,1,0:T(8,128)(2,1)} %pending_hbm.1, f32[1,2048]{1,0:T(1,128)} %gain_hbm.1, ...), custom_call_target="tpu_custom_call" | custom-call | tf_op jit(solution)/shard_map/pallas_call | solution.py:585
  28.0 32.9 %shard_map.140 = (bf16[1,128,1024]{2,1,0:T(8,128)(2,1)}, bf16[1,128,1024]{2,1,0:T(8,128)(2,1)}, f32[1,512,256]{2,1,0:T(8,128)}) custom-call(bf16[1,128,1024]{2,1,0:T(8,128)(2,1)} %get-tuple-element.6.refs_0_, bf16[1,128,1024]{2,1,0:T(8,128)(2,1)} %get-tuple-element.7.refs_1_, f32[1,512,256]{2,1,0:T(8,128)} %get-tuple-element.8.refs_2_), custom_call_target="tpu_custom_call" | custom-call | tf_op jit(solution)/shard_map/pallas_call | solution.py:612

commit v3 on v2

--- a/solution.py
+++ b/solution.py
@@ -10,6 +10,7 @@
 
 HEAD_WIDTH = 128
 CHUNK = 256
+STORE_BLOCKS = 2
 EPSILON = 1e-06
 F32 = jnp.float32
 BF16 = jnp.bfloat16
@@ -122,17 +123,22 @@
 
     x_load = local(x_hbm.at[0], x1.at[me], local_sem.at[0])
     gain_load = local(gain_hbm, gain, local_sem.at[1])
-    wk_load = local(wk_hbm.at[0], wk, weight_sem.at[0])
-    wv_load = local(wv_hbm.at[0], wv, weight_sem.at[1])
-    quarter = model // 4
-    wq_loads = [
-        local(
-            wq_hbm.at[0, pl.ds(i * quarter, quarter)],
-            wq.at[pl.ds(i * quarter, quarter)],
-            weight_sem.at[2 + i],
-        )
-        for i in range(4)
-    ]
+    weight_loads = []
+    for step in range(heads):
+        first = pl.multiple_of(lax.rem(me + heads - step, heads) * width, CHUNK)
+        half = width // 2
+        blocks = [(wk_hbm, wk, first, width), (wv_hbm, wv, first, width)]
+        blocks += [(wq_hbm, wq, first + i * half, half) for i in range(2)]
+        weight_loads.append(
+            [
+                local(
+                    source.at[0, pl.ds(pl.multiple_of(row, CHUNK), size)],
+                    target.at[pl.ds(pl.multiple_of(row, CHUNK), size)],
+                    weight_sem.at[4 * step + i],
+                )
+                for i, (source, target, row, size) in enumerate(blocks)
+            ]
+        )
     seg_load = local(seg_hbm, seg, local_sem.at[2])
     scale_load = local(scale_hbm, scale, local_sem.at[3])
     blend_load = local(blend_hbm, blend, local_sem.at[4])
@@ -143,11 +149,12 @@
     def _():
         f1_load.start()
 
+    quarter = model // 4
     wo_loads = [
         local(
             wo_hbm.at[0, pl.ds(i * quarter, quarter)],
             wo.at[pl.ds(i * quarter, quarter)],
-            weight_sem.at[6 + i],
+            weight_sem.at[4 * heads + i],
         )
         for i in range(4)
     ]
@@ -252,9 +259,7 @@
 
     gain_load.wait()
     x_load.wait()
-    wk_load.wait()
-    wv_load.wait()
-    for load in wq_loads:
+    for load in weight_loads[0]:
         load.wait()
     part = x1[me].astype(F32)
     squares = jnp.sum(part * part, axis=-1, keepdims=True)
@@ -267,6 +272,8 @@
     inverse1 = normalize(x1, squares, normed1)
     n1_copies = send_normed(normed1, 0)
     for step in range(1, heads):
+        for load in weight_loads[step]:
+            load.wait()
         owner = lax.rem(me + heads - step, heads)
         project(x1[owner].astype(F32), owner * width, width, False)
 
@@ -498,19 +505,25 @@
 
 
 def store_kernel(*refs):
-    sources, targets, sems = refs[:3], refs[3:6], refs[6]
-    copies = []
-    for source, target in zip(sources, targets):
-        rows = source.shape[1] // 2
-        for i in range(2):
-            block = pl.ds(i * rows, rows)
-            copy = pltpu.make_async_copy(
-                source.at[0, block], target.at[0, block], sems.at[len(copies)]
+    sources, targets, buffers, load_sem, store_sem = refs[:3], refs[3:6], refs[6:9], refs[9], refs[10]
+    loads, stores = [], []
+    for source, target, buffer in zip(sources, targets, buffers):
+        rows = source.shape[1] // STORE_BLOCKS
+        for i in range(STORE_BLOCKS):
+            block, n = pl.ds(i * rows, rows), len(loads)
+            loads.append(
+                pltpu.make_async_copy(source.at[0, block], buffer.at[block], load_sem.at[n])
             )
-            copy.start()
-            copies.append(copy)
-    for copy in copies:
-        copy.wait()
+            stores.append(
+                pltpu.make_async_copy(buffer.at[block], target.at[0, block], store_sem.at[n])
+            )
+    for load in loads:
+        load.start()
+    for load, store in zip(loads, stores):
+        load.wait()
+        store.start()
+    for store in stores:
+        store.wait()
 
 
 def solution(mesh):
@@ -564,7 +577,7 @@
             pltpu.VMEM((replicas, 2, tokens, kv_width), BF16),
             pltpu.VMEM((grad_rows, kv_width), F32),
             dma((7,)),
-            dma((10,)),
+            dma((4 * heads + 4,)),
             dma((heads,)),
             dma((3,)),
             dma((others,)),
@@ -614,7 +627,8 @@
             out_shape=tuple(jax.ShapeDtypeStruct(r.shape, r.dtype) for r in results),
             in_specs=[pl.BlockSpec(memory_space=pl.ANY)] * 3,
             out_specs=(pl.BlockSpec(memory_space=pl.ANY),) * 3,
-            scratch_shapes=[dma((6,))],
+            scratch_shapes=[pltpu.VMEM(r.shape[1:], r.dtype) for r in results]
+            + [dma((3 * STORE_BLOCKS,)), dma((3 * STORE_BLOCKS,))],
             compiler_params=pltpu.CompilerParams(vmem_limit_bytes=56 * 1024 * 1024),
         )(*results)
 

time: 61.1 us -> 30.3 us (0.50)
  Pallas kernels: 60.3 us -> 29.5 us
    pallas_call x1, Pallas kernels: 32.9 us -> 2.1 us  [per_device(): pl.pallas_call(store_kernel, out_shape=tuple((jax.ShapeDtypeStruct(r.shap...]
where the time goes in v3:
time: 30.3 us; the launch traced here: 30.2 us
  Pallas kernels  29.5 us (97%)
  between operations  0.64 us (2%)
    pallas_call x1, Pallas kernels, per_device(): pl.pallas_call(functools.partial(kernel, sections, replicas, heads), out_...  27.4 us
    pallas_call x1, Pallas kernels, per_device(): pl.pallas_call(store_kernel, out_shape=tuple((jax.ShapeDtypeStruct(r.shap...  2.1 us

profile of v3, /device:TPU:17, one launch (start us, length us, event | category | flops | bytes accessed | tf_op | source)
XLA Modules:
  0.0 30.2 jit_solution(5350397316853948764)
XLA Ops:
  0.6 27.4 %shard_map.139 = (bf16[1,128,1024]{2,1,0:T(8,128)(2,1)}, bf16[1,128,1024]{2,1,0:T(8,128)(2,1)}, f32[1,512,256]{2,1,0:T(8,128)}) custom-call(s32[5,128]{1,0:T(8,128)} %seg_hbm.1, bf16[1,128,1024]{2,1,0:T(8,128)(2,1)} %x_hbm.1, bf16[128,2048]{1,0:T(8,128)(2,1)} %entering_hbm.1, bf16[1,128,256]{2,1,0:T(8,128)(2,1)} %pending_hbm.1, f32[1,2048]{1,0:T(1,128)} %gain_hbm.1, ...), custom_call_target="tpu_custom_call" | custom-call | tf_op jit(solution)/shard_map/pallas_call | solution.py:598
  28.1 2.1 %shard_map.140 = (bf16[1,128,1024]{2,1,0:T(8,128)(2,1)}, bf16[1,128,1024]{2,1,0:T(8,128)(2,1)}, f32[1,512,256]{2,1,0:T(8,128)}) custom-call(bf16[1,128,1024]{2,1,0:T(8,128)(2,1)} %get-tuple-element.6.refs_0_, bf16[1,128,1024]{2,1,0:T(8,128)(2,1)} %get-tuple-element.7.refs_1_, f32[1,512,256]{2,1,0:T(8,128)} %get-tuple-element.8.refs_2_), custom_call_target="tpu_custom_call" | custom-call | tf_op jit(solution)/shard_map/pallas_call | solution.py:625

commit v4 on v3

--- a/solution.py
+++ b/solution.py
@@ -222,11 +222,15 @@
     k_at, v_at = q_width, q_width + kv_width
     weights_at = ((wk, k_at, kv_width), (wv, v_at, kv_width), (wq, 0, q_width))
 
-    def project(part, first_row, size, is_start):
-        rows = pl.ds(pl.multiple_of(first_row, CHUNK), size)
-        scaled = (part * gain[:, rows]).astype(BF16)
+    def project(pieces, size, is_start):
+        scaled = []
+        for part, first_row in pieces:
+            rows = pl.ds(pl.multiple_of(first_row, CHUNK), size)
+            scaled.append(((part * gain[:, rows]).astype(BF16), rows))
         for weight, at, columns in weights_at:
-            product = dot(scaled, weight[rows, :])
+            product = dot(scaled[0][0], weight[scaled[0][1], :])
+            for piece, rows in scaled[1:]:
+                product += dot(piece, weight[rows, :])
             if is_start:
                 acc[:, pl.ds(at, columns)] = product
             else:
@@ -263,7 +267,7 @@
         load.wait()
     part = x1[me].astype(F32)
     squares = jnp.sum(part * part, axis=-1, keepdims=True)
-    project(part, me * width, width, True)
+    project([(part, me * width)], width, True)
     for copy in x_copies:
         copy.wait_recv()
     for step in range(1, heads):
@@ -275,7 +279,7 @@
         for load in weight_loads[step]:
             load.wait()
         owner = lax.rem(me + heads - step, heads)
-        project(x1[owner].astype(F32), owner * width, width, False)
+        project([(x1[owner].astype(F32), owner * width)], width, False)
 
     seg_load.wait()
     scale_load.wait()
@@ -308,51 +312,54 @@
         row = seg[pl.ds(segment_index, 1), :].astype(F32)
         across = jnp.broadcast_to(row, (tokens, tokens))
         allowed = causal & (across == across.T)
+        queries, keys, mixes = [], [], []
         for g in range(kv_heads):
             kv_columns = pl.ds(g * HEAD_WIDTH, HEAD_WIDTH)
             values = acc[:, pl.ds(v_at + g * HEAD_WIDTH, HEAD_WIDTH)] * inverse
             blended = values + blend[:, g : g + 1] * earlier[:, kv_columns].astype(F32)
             mixed_values = jnp.where(is_first, values, blended).astype(BF16)
-            key_high, key_low = split_high_low(
-                unit_rows(acc[:, pl.ds(k_at + g * HEAD_WIDTH, HEAD_WIDTH)] * inverse)
-            )
-            keys = jnp.concatenate([key_high, key_high, key_low], axis=1)
-            queries = []
+            mixes.append(jnp.concatenate([mixed_values, mixed_ones], axis=1))
+            stacked = [acc[:, pl.ds(k_at + g * HEAD_WIDTH, HEAD_WIDTH)] * inverse]
+            for h in range(g * group, (g + 1) * group):
+                stacked.append(acc[:, pl.ds(h * HEAD_WIDTH, HEAD_WIDTH)] * inverse)
+            unit = unit_rows(jnp.concatenate(stacked, axis=0))
+            key_high, key_low = split_high_low(unit[:tokens])
+            keys.append(jnp.concatenate([key_high, key_high, key_low], axis=1))
+            parts = []
             for j in range(group):
                 h = g * group + j
                 query_high, query_low = split_high_low(
-                    unit_rows(acc[:, pl.ds(h * HEAD_WIDTH, HEAD_WIDTH)] * inverse)
+                    unit[(j + 1) * tokens : (j + 2) * tokens]
                     * (scale[:, h : h + 1] / math.sqrt(HEAD_WIDTH))
                 )
-                queries.append(jnp.concatenate([query_high, query_low, query_high], axis=1))
-            scores = lax.dot_general(
-                jnp.concatenate(queries, axis=0),
-                keys,
-                (((1,), (1,)), ((), ())),
-                preferred_element_type=F32,
-            ).reshape(group, tokens, tokens)
-            scores = jnp.where(allowed[None], scores, -1e30)
-            exponent = jnp.exp(scores - jnp.max(scores, axis=-1, keepdims=True)).astype(BF16)
-            result = dot(
-                exponent.reshape(group * tokens, tokens),
-                jnp.concatenate([mixed_values, mixed_ones], axis=1),
-            )
+                parts.append(jnp.concatenate([query_high, query_low, query_high], axis=1))
+            queries.append(jnp.concatenate(parts, axis=0))
+        scores = [
+            lax.dot_general(q, k, (((1,), (1,)), ((), ())), preferred_element_type=F32)
+            for q, k in zip(queries, keys)
+        ]
+        exponents = []
+        for score in scores:
+            score = jnp.where(allowed[None], score.reshape(group, tokens, tokens), -1e30)
+            top = jnp.max(score, axis=-1, keepdims=True)
+            exponents.append(jnp.exp(score - top).astype(BF16).reshape(group * tokens, tokens))
+        results = [dot(e, m) for e, m in zip(exponents, mixes)]
+        for g, result in enumerate(results):
             result = (result[:, :HEAD_WIDTH] / result[:, HEAD_WIDTH:]).astype(BF16)
             for j in range(group):
                 att[me, :, pl.ds((g * group + j) * HEAD_WIDTH, HEAD_WIDTH)] = result[
                     j * tokens : (j + 1) * tokens
                 ]
-            columns = pl.ds(g * group * HEAD_WIDTH, group * HEAD_WIDTH)
-            for step in range(1, heads):
-                copy = remote(
-                    att.at[me, :, columns],
-                    att.at[me, :, columns],
-                    a_send.at[turn, step - 1, g],
-                    a_recv.at[turn, step - 1, g],
-                    (section, replica, head_at(step)),
-                )
-                copy.start()
-                a_copies.append((turn, copy))
+        for step in range(1, heads):
+            copy = remote(
+                att.at[me],
+                att.at[me],
+                a_send.at[turn, step - 1],
+                a_recv.at[turn, step - 1],
+                (section, replica, head_at(step)),
+            )
+            copy.start()
+            a_copies.append((turn, copy))
 
     a_copies = []
     attend(section, f1, att1, 0, inverse1)
@@ -400,17 +407,14 @@
 
     out1_store = local(out1, out1_hbm.at[0], out_sem.at[0])
 
-    def grad_part(turn, step):
-        p = lax.rem(replica + replicas - step, replicas)
+    def grad_part(turn):
+        features = jnp.concatenate([rows_n[turn, p] for p in range(replicas)], axis=0)
+        cotangents = jnp.concatenate([rows_c[p, turn] for p in range(replicas)], axis=0)
         return lax.dot_general(
-            rows_n[turn, p],
-            rows_c[p, turn],
-            (((0,), (0,)), ((), ())),
-            preferred_element_type=F32,
+            features, cotangents, (((0,), (0,)), ((), ())), preferred_element_type=F32
         )
 
     cot_load.wait()
-    grad[...] = grad_part(0, 0)
 
     def forward(step, c):
         columns = pl.ds(c * CHUNK, CHUNK)
@@ -428,38 +432,33 @@
             load.wait()
 
     squares = jnp.zeros((tokens, 1), F32)
-    for c in range(chunks):
-        columns = pl.ds(c * CHUNK, CHUNK)
-
+    for c in range(chunks + 1):
         @pl.when(not_first)
         def _(c=c):
-            z_copy(c).wait_recv()
-            for step in range(1, heads):
-                forward(step, c).start()
-
-        part = x2[me, :, columns].astype(F32)
-        squares += jnp.sum(part * part, axis=-1, keepdims=True)
-        project(part, me * width + c * CHUNK, CHUNK, c == 0)
-        if c < chunks - 1:
-            for step in range(1 + c * (replicas - 1) // (chunks - 1), 1 + (c + 1) * (replicas - 1) // (chunks - 1)):
-                c_copies[step - 1].wait_recv()
-                n1_copies[step - 1].wait_recv()
-                grad[...] += grad_part(0, step)
-
-        @pl.when(not_first)
-        def _(c=c):
-            for step in range(1, heads):
-                forward(step, c).wait_recv()
-
-        parts = [x2[lax.rem(me + heads - step, heads), :, columns].astype(F32) for step in range(1, heads)]
-        for part in parts:
-            squares += jnp.sum(part * part, axis=-1, keepdims=True)
-        if c == chunks - 1:
+            if c < chunks:
+                z_copy(c).wait_recv()
+                for step in range(1, heads):
+                    forward(step, c).start()
+            if c > 0:
+                for step in range(1, heads):
+                    forward(step, c - 1).wait_recv()
+
+        pieces = []
+        for step in range(heads):
+            at = c if step == 0 else c - 1
+            if 0 <= at < chunks:
+                owner = lax.rem(me + heads - step, heads)
+                part = x2[owner, :, pl.ds(at * CHUNK, CHUNK)].astype(F32)
+                squares += jnp.sum(part * part, axis=-1, keepdims=True)
+                pieces.append((part, owner * width + at * CHUNK))
+        if c == chunks:
             inverse2 = normalize(x2, squares, normed2)
             n2_copies = send_normed(normed2, 1)
-        for step in range(1, heads):
-            owner = lax.rem(me + heads - step, heads)
-            project(parts[step - 1], owner * width + c * CHUNK, CHUNK, False)
+        project(pieces, CHUNK, c == 0)
+        if c == chunks - 2:
+            for copy in c_copies + n1_copies:
+                copy.wait_recv()
+            grad[...] = grad_part(0)
 
     @pl.when(not_first)
     def _():
@@ -475,11 +474,9 @@
         out2[:, pl.ds(c * CHUNK, CHUNK)] = whole_tile(att2, x2, c)
     out2_store = local(out2, out2_hbm.at[0], out_sem.at[1])
 
-    total = grad[...] + grad_part(1, 0)
-    for step in range(1, replicas):
-        n2_copies[step - 1].wait_recv()
-        total += grad_part(1, step)
-    grad[...] = total
+    for copy in n2_copies:
+        copy.wait_recv()
+    grad[...] += grad_part(1)
     grad_store = local(grad, grad_hbm.at[0], out_sem.at[2])
 
     for copy in x_copies + c_copies + n1_copies + n2_copies:
@@ -548,7 +545,6 @@
         q_width, kv_width = wq.shape[2], wk.shape[2]
         grad_rows = model // replicas
         chunks = width // CHUNK
-        kv_heads = kv_width // HEAD_WIDTH
         others = heads - 1
         peers = replicas - 1
         dma = pltpu.SemaphoreType.DMA
@@ -586,8 +582,8 @@
             dma((peers,)),
             dma((2, peers)),
             dma((2, peers)),
-            dma((2, others, kv_heads)),
-            dma((2, others, kv_heads)),
+            dma((2, others)),
+            dma((2, others)),
             dma((chunks,)),
             dma((chunks,)),
             dma((others, chunks)),

time: 30.3 us -> 29.8 us (0.983)
  Pallas kernels: 29.5 us -> 29 us
    pallas_call x1, Pallas kernels: 27.4 us -> 26.9 us  [per_device(): pl.pallas_call(functools.partial(kernel, sections, replicas, heads), out_...]
where the time goes in v4:
time: 29.8 us; the launch traced here: 29.6 us
  Pallas kernels  29 us (97%)
  between operations  0.64 us (2%)
    pallas_call x1, Pallas kernels, per_device(): pl.pallas_call(functools.partial(kernel, sections, replicas, heads), out_...  26.9 us
    pallas_call x1, Pallas kernels, per_device(): pl.pallas_call(store_kernel, out_shape=tuple((jax.ShapeDtypeStruct(r.shap...  2.1 us

profile of v4, /device:TPU:17, one launch (start us, length us, event | category | flops | bytes accessed | tf_op | source)
XLA Modules:
  0.0 29.6 jit_solution(7891012134004071834)
XLA Ops:
  0.6 26.9 %shard_map.139 = (bf16[1,128,1024]{2,1,0:T(8,128)(2,1)}, bf16[1,128,1024]{2,1,0:T(8,128)(2,1)}, f32[1,512,256]{2,1,0:T(8,128)}) custom-call(s32[5,128]{1,0:T(8,128)} %seg_hbm.1, bf16[1,128,1024]{2,1,0:T(8,128)(2,1)} %x_hbm.1, bf16[128,2048]{1,0:T(8,128)(2,1)} %entering_hbm.1, bf16[1,128,256]{2,1,0:T(8,128)(2,1)} %pending_hbm.1, f32[1,2048]{1,0:T(1,128)} %gain_hbm.1, ...), custom_call_target="tpu_custom_call" | custom-call | tf_op jit(solution)/shard_map/pallas_call | solution.py:594
  27.5 2.1 %shard_map.140 = (bf16[1,128,1024]{2,1,0:T(8,128)(2,1)}, bf16[1,128,1024]{2,1,0:T(8,128)(2,1)}, f32[1,512,256]{2,1,0:T(8,128)}) custom-call(bf16[1,128,1024]{2,1,0:T(8,128)(2,1)} %get-tuple-element.6.refs_0_, bf16[1,128,1024]{2,1,0:T(8,128)(2,1)} %get-tuple-element.7.refs_1_, f32[1,512,256]{2,1,0:T(8,128)} %get-tuple-element.8.refs_2_), custom_call_target="tpu_custom_call" | custom-call | tf_op jit(solution)/shard_map/pallas_call | solution.py:621

commit v5 on v4

--- a/solution.py
+++ b/solution.py
@@ -85,6 +85,8 @@
     f_recv,
     v_send,
     v_recv,
+    h_send,
+    h_recv,
 ):
     section = lax.axis_index("section")
     replica = lax.axis_index("dp")
@@ -243,14 +245,34 @@
             normed[:, columns] = (stream[h].astype(F32) * inverse * gain[:, columns]).astype(BF16)
         return inverse
 
+    share_rows = tokens // heads
+    share = pl.ds(pl.multiple_of(me * share_rows, share_rows), share_rows)
+
+    def hand_on(copies, turn):
+        handed = []
+        for step in range(1, replicas):
+            copies[step - 1].wait_recv()
+            block = rows_n.at[turn, lax.rem(replica + replicas - step, replicas), share]
+            for hop in range(1, heads):
+                copy = remote(
+                    block,
+                    block,
+                    h_send.at[turn, step - 1, hop - 1],
+                    h_recv.at[turn, step - 1, hop - 1],
+                    (section, replica, head_at(hop)),
+                )
+                copy.start()
+                handed.append(copy)
+        return handed
+
     def send_normed(normed, turn):
         copies = []
         for step in range(1, replicas):
             peer = replica_at(step)
             first = pl.multiple_of(peer * grad_rows, 128)
             copy = remote(
-                normed.at[:, pl.ds(first, grad_rows)],
-                rows_n.at[turn, replica],
+                normed.at[share, pl.ds(first, grad_rows)],
+                rows_n.at[turn, replica, share],
                 n_send.at[turn, step - 1],
                 n_recv.at[turn, step - 1],
                 (section, peer, me),
@@ -456,7 +478,9 @@
             n2_copies = send_normed(normed2, 1)
         project(pieces, CHUNK, c == 0)
         if c == chunks - 2:
-            for copy in c_copies + n1_copies:
+            handed1 = hand_on(n1_copies, 0)
+        if c == chunks - 1:
+            for copy in c_copies + handed1:
                 copy.wait_recv()
             grad[...] = grad_part(0)
 
@@ -471,15 +495,17 @@
         if turn == 1:
             copy.wait_recv()
     for c in range(chunks):
+        if c == chunks // 2:
+            handed2 = hand_on(n2_copies, 1)
         out2[:, pl.ds(c * CHUNK, CHUNK)] = whole_tile(att2, x2, c)
     out2_store = local(out2, out2_hbm.at[0], out_sem.at[1])
 
-    for copy in n2_copies:
+    for copy in handed2:
         copy.wait_recv()
     grad[...] += grad_part(1)
     grad_store = local(grad, grad_hbm.at[0], out_sem.at[2])
 
-    for copy in x_copies + c_copies + n1_copies + n2_copies:
+    for copy in x_copies + c_copies + n1_copies + n2_copies + handed1 + handed2:
         copy.wait_send()
     for _, copy in a_copies:
         copy.wait_send()
@@ -590,6 +616,8 @@
             dma((others, chunks)),
             dma((1,)),
             dma((1,)),
+            dma((2, peers, others)),
+            dma((2, peers, others)),
         ]
         results = pl.pallas_call(
             functools.partial(kernel, sections, replicas, heads),

time: 29.8 us -> 26.7 us (0.90)
  Pallas kernels: 29 us -> 25.9 us
    pallas_call x1, Pallas kernels: 26.9 us -> 23.8 us  [per_device(): pl.pallas_call(functools.partial(kernel, sections, replicas, heads), out_...]
where the time goes in v5:
time: 26.7 us; the launch traced here: 26.5 us
  Pallas kernels  25.9 us (97%)
  between operations  0.64 us (2%)
    pallas_call x1, Pallas kernels, per_device(): pl.pallas_call(functools.partial(kernel, sections, replicas, heads), out_...  23.8 us
    pallas_call x1, Pallas kernels, per_device(): pl.pallas_call(store_kernel, out_shape=tuple((jax.ShapeDtypeStruct(r.shap...  2.1 us

profile of v5, /device:TPU:17, one launch (start us, length us, event | category | flops | bytes accessed | tf_op | source)
XLA Modules:
  0.0 26.5 jit_solution(17591798093460853535)
XLA Ops:
  0.6 23.8 %shard_map.139 = (bf16[1,128,1024]{2,1,0:T(8,128)(2,1)}, bf16[1,128,1024]{2,1,0:T(8,128)(2,1)}, f32[1,512,256]{2,1,0:T(8,128)}) custom-call(s32[5,128]{1,0:T(8,128)} %seg_hbm.1, bf16[1,128,1024]{2,1,0:T(8,128)(2,1)} %x_hbm.1, bf16[128,2048]{1,0:T(8,128)(2,1)} %entering_hbm.1, bf16[1,128,256]{2,1,0:T(8,128)(2,1)} %pending_hbm.1, f32[1,2048]{1,0:T(1,128)} %gain_hbm.1, ...), custom_call_target="tpu_custom_call" | custom-call | tf_op jit(solution)/shard_map/pallas_call | solution.py:622
  24.4 2.1 %shard_map.140 = (bf16[1,128,1024]{2,1,0:T(8,128)(2,1)}, bf16[1,128,1024]{2,1,0:T(8,128)(2,1)}, f32[1,512,256]{2,1,0:T(8,128)}) custom-call(bf16[1,128,1024]{2,1,0:T(8,128)(2,1)} %get-tuple-element.6.refs_0_, bf16[1,128,1024]{2,1,0:T(8,128)(2,1)} %get-tuple-element.7.refs_1_, f32[1,512,256]{2,1,0:T(8,128)} %get-tuple-element.8.refs_2_), custom_call_target="tpu_custom_call" | custom-call | tf_op jit(solution)/shard_map/pallas_call | solution.py:649

commit v6 on v5

--- a/solution.py
+++ b/solution.py
@@ -209,17 +209,21 @@
         x_copies.append(copy)
     value_copy = remote(f1, f2, v_send.at[0], v_recv.at[0], (section + 1, replica, me))
 
-    c_copies = []
-    for step in range(1, replicas):
-        copy = remote(
-            cot_hbm.at[0],
-            rows_c.at[replica],
-            c_send.at[step - 1],
-            c_recv.at[step - 1],
-            (section, replica_at(step), me),
-        )
-        copy.start()
-        c_copies.append(copy)
+    def send_cotangents(turn):
+        copies = []
+        for step in range(1, replicas):
+            copy = remote(
+                cot_hbm.at[0, turn],
+                rows_c.at[replica, turn],
+                c_send.at[turn, step - 1],
+                c_recv.at[turn, step - 1],
+                (section, replica_at(step), me),
+            )
+            copy.start()
+            copies.append(copy)
+        return copies
+
+    c1_copies = send_cotangents(0)
 
     k_at, v_at = q_width, q_width + kv_width
     weights_at = ((wk, k_at, kv_width), (wv, v_at, kv_width), (wq, 0, q_width))
@@ -297,6 +301,7 @@
         squares += jnp.sum(part * part, axis=-1, keepdims=True)
     inverse1 = normalize(x1, squares, normed1)
     n1_copies = send_normed(normed1, 0)
+    c2_copies = send_cotangents(1)
     for step in range(1, heads):
         for load in weight_loads[step]:
             load.wait()
@@ -480,7 +485,7 @@
         if c == chunks - 2:
             handed1 = hand_on(n1_copies, 0)
         if c == chunks - 1:
-            for copy in c_copies + handed1:
+            for copy in c1_copies + handed1:
                 copy.wait_recv()
             grad[...] = grad_part(0)
 
@@ -500,12 +505,12 @@
         out2[:, pl.ds(c * CHUNK, CHUNK)] = whole_tile(att2, x2, c)
     out2_store = local(out2, out2_hbm.at[0], out_sem.at[1])
 
-    for copy in handed2:
+    for copy in c2_copies + handed2:
         copy.wait_recv()
     grad[...] += grad_part(1)
     grad_store = local(grad, grad_hbm.at[0], out_sem.at[2])
 
-    for copy in x_copies + c_copies + n1_copies + n2_copies + handed1 + handed2:
+    for copy in x_copies + c1_copies + c2_copies + n1_copies + n2_copies + handed1 + handed2:
         copy.wait_send()
     for _, copy in a_copies:
         copy.wait_send()
@@ -604,8 +609,8 @@
             dma((3,)),
             dma((others,)),
             dma((others,)),
-            dma((peers,)),
-            dma((peers,)),
+            dma((2, peers)),
+            dma((2, peers)),
             dma((2, peers)),
             dma((2, peers)),
             dma((2, others)),

time: 26.7 us -> 26.7 us (level)
  no operation moved by 1% of the time
where the time goes in v6:
time: 26.7 us; the launch traced here: 26.6 us
  Pallas kernels  25.9 us (97%)
  between operations  0.64 us (2%)
    pallas_call x1, Pallas kernels, per_device(): pl.pallas_call(functools.partial(kernel, sections, replicas, heads), out_...  23.8 us
    pallas_call x1, Pallas kernels, per_device(): pl.pallas_call(store_kernel, out_shape=tuple((jax.ShapeDtypeStruct(r.shap...  2.1 us

profile of v6, /device:TPU:17, one launch (start us, length us, event | category | flops | bytes accessed | tf_op | source)
XLA Modules:
  0.0 26.6 jit_solution(12312300062040691475)
XLA Ops:
  0.6 23.8 %shard_map.139 = (bf16[1,128,1024]{2,1,0:T(8,128)(2,1)}, bf16[1,128,1024]{2,1,0:T(8,128)(2,1)}, f32[1,512,256]{2,1,0:T(8,128)}) custom-call(s32[5,128]{1,0:T(8,128)} %seg_hbm.1, bf16[1,128,1024]{2,1,0:T(8,128)(2,1)} %x_hbm.1, bf16[128,2048]{1,0:T(8,128)(2,1)} %entering_hbm.1, bf16[1,128,256]{2,1,0:T(8,128)(2,1)} %pending_hbm.1, f32[1,2048]{1,0:T(1,128)} %gain_hbm.1, ...), custom_call_target="tpu_custom_call" | custom-call | tf_op jit(solution)/shard_map/pallas_call | solution.py:627
  24.5 2.1 %shard_map.140 = (bf16[1,128,1024]{2,1,0:T(8,128)(2,1)}, bf16[1,128,1024]{2,1,0:T(8,128)(2,1)}, f32[1,512,256]{2,1,0:T(8,128)}) custom-call(bf16[1,128,1024]{2,1,0:T(8,128)(2,1)} %get-tuple-element.6.refs_0_, bf16[1,128,1024]{2,1,0:T(8,128)(2,1)} %get-tuple-element.7.refs_1_, f32[1,512,256]{2,1,0:T(8,128)} %get-tuple-element.8.refs_2_), custom_call_target="tpu_custom_call" | custom-call | tf_op jit(solution)/shard_map/pallas_call | solution.py:654

commit v7 on v6

--- a/solution.py
+++ b/solution.py
@@ -417,7 +417,7 @@
 
     for load in wo_loads:
         load.wait()
-    ahead = chunks // 2
+    ahead = 1
     for c in range(ahead):
         own_tile(att1, c)
     for turn, copy in a_copies:

time: 26.7 us -> 26.7 us (level)
  no operation moved by 1% of the time
where the time goes in v7:
time: 26.7 us; the launch traced here: 26.6 us
  Pallas kernels  25.9 us (97%)
  between operations  0.64 us (2%)
    pallas_call x1, Pallas kernels, per_device(): pl.pallas_call(functools.partial(kernel, sections, replicas, heads), out_...  23.8 us
    pallas_call x1, Pallas kernels, per_device(): pl.pallas_call(store_kernel, out_shape=tuple((jax.ShapeDtypeStruct(r.shap...  2.1 us

profile of v7, /device:TPU:17, one launch (start us, length us, event | category | flops | bytes accessed | tf_op | source)
XLA Modules:
  0.0 26.6 jit_solution(10294176537948771793)
XLA Ops:
  0.6 23.8 %shard_map.139 = (bf16[1,128,1024]{2,1,0:T(8,128)(2,1)}, bf16[1,128,1024]{2,1,0:T(8,128)(2,1)}, f32[1,512,256]{2,1,0:T(8,128)}) custom-call(s32[5,128]{1,0:T(8,128)} %seg_hbm.1, bf16[1,128,1024]{2,1,0:T(8,128)(2,1)} %x_hbm.1, bf16[128,2048]{1,0:T(8,128)(2,1)} %entering_hbm.1, bf16[1,128,256]{2,1,0:T(8,128)(2,1)} %pending_hbm.1, f32[1,2048]{1,0:T(1,128)} %gain_hbm.1, ...), custom_call_target="tpu_custom_call" | custom-call | tf_op jit(solution)/shard_map/pallas_call | solution.py:627
  24.5 2.1 %shard_map.140 = (bf16[1,128,1024]{2,1,0:T(8,128)(2,1)}, bf16[1,128,1024]{2,1,0:T(8,128)(2,1)}, f32[1,512,256]{2,1,0:T(8,128)}) custom-call(bf16[1,128,1024]{2,1,0:T(8,128)(2,1)} %get-tuple-element.6.refs_0_, bf16[1,128,1024]{2,1,0:T(8,128)(2,1)} %get-tuple-element.7.refs_1_, f32[1,512,256]{2,1,0:T(8,128)} %get-tuple-element.8.refs_2_), custom_call_target="tpu_custom_call" | custom-call | tf_op jit(solution)/shard_map/pallas_call | solution.py:654
